TPU v7x, 32 devices: a whole 2x2x4 slice. The times are simulated.
32 devices in a mesh: cases: 2 (over x), azim: 16 (over z, y, core).
Axes of the slice: x: 2, y: 2, z: 4, core: 2. Of those that a mesh axis runs over, the one named last changes fastest.
Arguments:
- wake: float32 [3, 32, 32, 128], P(None, ('cases', 'azim')), parts along dimension 1
- release: float32 [3, 32, 128], P(None, ('cases', 'azim')), parts along dimension 1
- strength: float32 [32, 128], P(('cases', 'azim')), parts along dimension 0, may hold values from -6 to 6
- source_list: int32 [32, 32, 8], P(('cases', 'azim')), parts along dimension 0, may hold values from 0 to 511, as said below
- list_count: int32 [32, 32], P(('cases', 'azim')), parts along dimension 0, may hold values from 1 to 8, as said below
Outputs:
- relaxed: float32 [3, 32, 32, 128], P(None, ('cases', 'azim')), parts along dimension 1
- induced: float32 [3, 32, 32, 128], P(None, ('cases', 'azim')), parts along dimension 1
There are 2 independent parts, one for each index of `cases`. A program takes and returns all parts, laid end to end along the dimension named above; each array names one. Nothing has to cross between parts.
Inputs may be any that keep to these rules, and one draw needn't show every extreme that they name: `source_list`: every listed tile lies in an azimuth block of 1 step that is -1 to 0 blocks, cyclically, from the target tile's block; slots at or past the tile's count hold valid ids too. `list_count`: some tile holds 8.
All inputs are finite; a program needn't handle non-finite values.
Results may differ from a plain program's by a relative error of at most 0.0001.
Values sent between devices are 32-bit elements; how exact they have to be, the bound alone decides.
A program may use at most 64 MiB of HBM per device.

v0:
```python
import math

import jax
import jax.numpy as jnp
from jax import lax
from jax.sharding import PartitionSpec as P

SWEEPS = 2


core_square = 0.01


def shifted(block, axis, distance):
    devices = range(lax.axis_size(axis))
    route = [((i - distance) % len(devices), i) for i in devices]
    return lax.ppermute(block, axis, route)


def segments(coords, strength):
    following = jnp.concatenate([coords[:, :, 1:, :], coords[:, :, -1:, :]], axis=2)
    middles = 0.5 * (coords + following)
    levers = (following - coords) * (strength[None, :, None, :] * (0.25 / math.pi))
    return (middles, levers)


def induce(points, middles, levers, active):
    delta_one = points[0][:, None, :, None] - middles[0][:, :, None, :]
    delta_two = points[1][:, None, :, None] - middles[1][:, :, None, :]
    delta_three = points[2][:, None, :, None] - middles[2][:, :, None, :]
    inverse = lax.rsqrt(
        delta_one * delta_one + delta_two * delta_two + delta_three * delta_three + core_square
    )
    weight = inverse * inverse * inverse * active[:, :, None, None]
    lever_one = levers[0][:, :, None, :]
    lever_two = levers[1][:, :, None, :]
    lever_three = levers[2][:, :, None, :]
    swirl_one = jnp.sum((lever_two * delta_three - lever_three * delta_two) * weight, axis=(1, 3))
    swirl_two = jnp.sum((lever_three * delta_one - lever_one * delta_three) * weight, axis=(1, 3))
    swirl_three = jnp.sum((lever_one * delta_two - lever_two * delta_one) * weight, axis=(1, 3))
    return jnp.stack([swirl_one, swirl_two, swirl_three])


def shift_local(coords, edge_pos, boundary):
    rolled = jnp.concatenate([edge_pos, coords[:, :-1]], axis=1)
    return jnp.concatenate([boundary[:, :, None, :], rolled[:, :, :-1, :]], axis=2)


def gather_window(coords, strength, reach_blocks):
    psi_local = coords.shape[1]
    if reach_blocks > 1:
        first_block = shifted((coords, strength), "azim", -(reach_blocks - 1))
    else:
        first_block = (coords, strength)
    width_cols = 2 * reach_blocks * psi_local
    pos_buffer = jnp.zeros((3, width_cols) + coords.shape[2:], jnp.float32)
    str_buffer = jnp.zeros((width_cols, strength.shape[1]), jnp.float32)
    pos_buffer = lax.dynamic_update_slice_in_dim(pos_buffer, first_block[0], 0, axis=1)
    str_buffer = lax.dynamic_update_slice_in_dim(str_buffer, first_block[1], 0, axis=0)

    def advance(hop_index, carry):
        current, pos_now, str_now = carry
        current = shifted((current[0], current[1]), "azim", 1)
        pos_now = lax.dynamic_update_slice_in_dim(
            pos_now, current[0], hop_index * psi_local, axis=1
        )
        str_now = lax.dynamic_update_slice_in_dim(
            str_now, current[1], hop_index * psi_local, axis=0
        )
        return (current, pos_now, str_now)

    result = lax.fori_loop(1, 2 * reach_blocks, advance, (first_block, pos_buffer, str_buffer))
    return (result[1], result[2])


def on_device(wake, release, strength, source_list, list_count):
    device_count = lax.axis_size("azim")
    reach_blocks = device_count // 16
    own_index = lax.axis_index("azim")
    psi_local = wake.shape[1]
    age_count = wake.shape[2]
    slot_count = source_list.shape[2]
    blocks = psi_local * age_count // 8
    column = source_list // age_count
    age_part = source_list % age_count
    owner_block = column // psi_local
    within = column % psi_local
    offset = (owner_block - own_index + reach_blocks) % device_count - reach_blocks
    local_ids = ((reach_blocks - 1 - offset) * psi_local + within) * age_count + age_part
    indices = local_ids.reshape(blocks, 8, slot_count)
    block_counts = list_count.reshape(blocks, 8)
    active = (
        jnp.arange(slot_count, dtype=jnp.int32)[None, None, :] < block_counts[:, :, None]
    ).astype(jnp.float32)
    drift = jnp.array([0.0, 0.0, -0.2], dtype=jnp.float32)[:, None, None, None]

    def velocity(coords):
        win_pos, win_str = gather_window(coords, strength, reach_blocks)
        middles, levers = segments(win_pos, win_str)
        window_tiles = win_pos.shape[1] * age_count
        flat_mid = middles.reshape(3, window_tiles, 128)
        flat_lever = levers.reshape(3, window_tiles, 128)
        targets = coords.reshape(3, blocks, 8, 128).transpose(1, 0, 2, 3)

        def one_block(packed):
            points, picked, weights = packed
            chosen_mid = jnp.take(flat_mid, picked.reshape(-1), axis=1).reshape(
                3, 8, slot_count, 128
            )
            chosen_lever = jnp.take(flat_lever, picked.reshape(-1), axis=1).reshape(
                3, 8, slot_count, 128
            )
            return induce(points, chosen_mid, chosen_lever, weights)

        swirling = lax.map(one_block, (targets, indices, active))
        swirling = swirling.transpose(1, 0, 2, 3).reshape(coords.shape)
        return swirling + drift

    positions = wake
    induced = jnp.zeros_like(wake)
    for sweep_index in range(SWEEPS):
        speed_now = velocity(positions)
        edge_pos, edge_speed = shifted((positions, speed_now), "azim", 1)
        back_pos = shift_local(positions, edge_pos, release)
        back_speed = shift_local(speed_now, edge_speed, jnp.zeros_like(release))
        predicted = back_pos + 0.05 * back_speed
        induced = velocity(predicted)
        corrected = back_pos + 0.025 * (back_speed + induced)
        positions = positions + 0.5 * (corrected - positions)
    return (positions, induced)


def solution(mesh):
    placed = (
        P(None, ("cases", "azim"), None, None),
        P(None, ("cases", "azim"), None),
        P(("cases", "azim"), None),
        P(("cases", "azim"), None, None),
        P(("cases", "azim"), None),
    )
    return jax.shard_map(
        on_device,
        mesh=mesh,
        in_specs=placed,
        out_specs=(P(None, ("cases", "azim"), None, None), P(None, ("cases", "azim"), None, None)),
        check_vma=False,
    )
```

profile of v0, /device:TPU:0, one launch (start us, length us, event | category | flops | bytes accessed | tf_op | source)
XLA Modules:
  0.0 158.3 jit_solution(6408357779408254447)
XLA Ops:
  9.2 29.3 %while.8 = (s32[]{:T(128)}, f32[4,3,8,128]{3,2,1,0:T(8,128)S(1)}, s32[4,8,8]{2,1,0:T(8,128)S(1)}, f32[3,64,128]{2,0,1:T(4,128)S(1)}, f32[4,3,8,128]{3,2,0,1:T(8,...) while((s32[]{:T(128)}, f32[4,3,8,128]{3,2,1,0:T(8,128)S(1)}, ...), condition=%wide.region_4.6_spmd, body=%wide.region_0.0_spmd.sunk | while | flops 28365376 | bytes 1482213 | solution.py:115
  11.0 5.5 %fusion.113 = (f32[8,128]{1,0:T(8,128)S(1)}, f32[8,128]{1,0:T(8,128)S(1)}, f32[8,128]{1,0:T(8,128)S(1)}) fusion(f32[8,8,128]{2,1,0:T(8,128)S(1)} %bitcast.298, f32[8,128]{1,0:T(8,128)S(1)} %get-tuple-element.627, f32[8,8,128]{2,1,0:T(8,128)S(1)} %bitcast.295, f32[8,8,128]{2,1,0:T(8,128)S(1)} %bitcast.297, f32[8,128]{1,0:T(8,128)S(1)} %get-tuple-element.630, ...), kind=kLoop, calls=%fused_computation.21.clone.1 | loop fusion | flops 28308480 | bytes 221440 | tf_op jit(solution)/shard_map/while/body/eval_jaxpr/reduce_sum | solution.py:38
  18.3 5.5 %fusion.113 = (f32[8,128]{1,0:T(8,128)S(1)}, f32[8,128]{1,0:T(8,128)S(1)}, f32[8,128]{1,0:T(8,128)S(1)}) fusion(f32[8,8,128]{2,1,0:T(8,128)S(1)} %bitcast.298, f32[8,128]{1,0:T(8,128)S(1)} %get-tuple-element.627, f32[8,8,128]{2,1,0:T(8,128)S(1)} %bitcast.295, f32[8,8,128]{2,1,0:T(8,128)S(1)} %bitcast.297, f32[8,128]{1,0:T(8,128)S(1)} %get-tuple-element.630, ...), kind=kLoop, calls=%fused_computation.21.clone.1 | loop fusion | flops 28308480 | bytes 221440 | tf_op jit(solution)/shard_map/while/body/eval_jaxpr/reduce_sum | solution.py:38
  25.6 5.5 %fusion.113 = (f32[8,128]{1,0:T(8,128)S(1)}, f32[8,128]{1,0:T(8,128)S(1)}, f32[8,128]{1,0:T(8,128)S(1)}) fusion(f32[8,8,128]{2,1,0:T(8,128)S(1)} %bitcast.298, f32[8,128]{1,0:T(8,128)S(1)} %get-tuple-element.627, f32[8,8,128]{2,1,0:T(8,128)S(1)} %bitcast.295, f32[8,8,128]{2,1,0:T(8,128)S(1)} %bitcast.297, f32[8,128]{1,0:T(8,128)S(1)} %get-tuple-element.630, ...), kind=kLoop, calls=%fused_computation.21.clone.1 | loop fusion | flops 28308480 | bytes 221440 | tf_op jit(solution)/shard_map/while/body/eval_jaxpr/reduce_sum | solution.py:38
  33.0 5.5 %fusion.113 = (f32[8,128]{1,0:T(8,128)S(1)}, f32[8,128]{1,0:T(8,128)S(1)}, f32[8,128]{1,0:T(8,128)S(1)}) fusion(f32[8,8,128]{2,1,0:T(8,128)S(1)} %bitcast.298, f32[8,128]{1,0:T(8,128)S(1)} %get-tuple-element.627, f32[8,8,128]{2,1,0:T(8,128)S(1)} %bitcast.295, f32[8,8,128]{2,1,0:T(8,128)S(1)} %bitcast.297, f32[8,128]{1,0:T(8,128)S(1)} %get-tuple-element.630, ...), kind=kLoop, calls=%fused_computation.21.clone.1 | loop fusion | flops 28308480 | bytes 221440 | tf_op jit(solution)/shard_map/while/body/eval_jaxpr/reduce_sum | solution.py:38
  38.6 6.2 %collective-permute-done.2 = f32[3,1,32,128]{3,2,1,0:T(8,128)S(1)} collective-permute-done((f32[3,1,32,128]{3,2,1,0:T(8,128)S(1)}, f32[3,1,32,128]{3,2,1,0:T(8,128)S(1)}, u32[]{:S(2)}, u32[]{:S(2)}) %collective-permute-start.2) | collective-permute-done | bytes 49184 | tf_op jit(solution)/shard_map/ppermute | solution.py:17
  44.9 6.2 %collective-permute-done.3 = f32[3,1,32,128]{3,2,1,0:T(8,128)S(1)} collective-permute-done((f32[3,1,32,128]{3,2,1,0:T(8,128)S(1)}, f32[3,1,32,128]{3,2,1,0:T(8,128)S(1)}, u32[]{:S(2)}, u32[]{:S(2)}) %collective-permute-start.3) | collective-permute-done | bytes 49184 | tf_op jit(solution)/shard_map/while/body/eval_jaxpr/ppermute | solution.py:17
  51.3 28.9 %while.9 = (s32[]{:T(128)}, f32[4,3,8,128]{3,2,1,0:T(8,128)S(1)}, s32[4,8,8]{2,1,0:T(8,128)S(1)}, f32[3,64,128]{2,0,1:T(4,128)S(1)}, f32[4,3,8,128]{3,2,1,0:T(8,...) while((s32[]{:T(128)}, f32[4,3,8,128]{3,2,1,0:T(8,128)S(1)}, ...), condition=%wide.region_9.11_spmd, body=%wide.region_5.10_spmd.sunk | while | flops 28365380 | bytes 1457693 | solution.py:115
  53.1 5.4 %fusion.116 = (f32[8,128]{1,0:T(8,128)S(1)}, f32[8,128]{1,0:T(8,128)S(1)}, f32[8,128]{1,0:T(8,128)S(1)}) fusion(f32[8,8,128]{2,1,0:T(8,128)S(1)} %bitcast.280, f32[8,128]{1,0:T(8,128)S(1)} %get-tuple-element.648, f32[8,8,128]{2,1,0:T(8,128)S(1)} %bitcast.277, f32[8,8,128]{2,1,0:T(8,128)S(1)} %bitcast.279, f32[8,128]{1,0:T(8,128)S(1)} %get-tuple-element.651, ...), kind=kLoop, calls=%fused_computation.58.clone.1 | loop fusion | flops 28308480 | bytes 221440 | tf_op jit(solution)/shard_map/while/body/eval_jaxpr/reduce_sum | solution.py:38
  60.4 5.4 %fusion.116 = (f32[8,128]{1,0:T(8,128)S(1)}, f32[8,128]{1,0:T(8,128)S(1)}, f32[8,128]{1,0:T(8,128)S(1)}) fusion(f32[8,8,128]{2,1,0:T(8,128)S(1)} %bitcast.280, f32[8,128]{1,0:T(8,128)S(1)} %get-tuple-element.648, f32[8,8,128]{2,1,0:T(8,128)S(1)} %bitcast.277, f32[8,8,128]{2,1,0:T(8,128)S(1)} %bitcast.279, f32[8,128]{1,0:T(8,128)S(1)} %get-tuple-element.651, ...), kind=kLoop, calls=%fused_computation.58.clone.1 | loop fusion | flops 28308480 | bytes 221440 | tf_op jit(solution)/shard_map/while/body/eval_jaxpr/reduce_sum | solution.py:38
  67.6 5.4 %fusion.116 = (f32[8,128]{1,0:T(8,128)S(1)}, f32[8,128]{1,0:T(8,128)S(1)}, f32[8,128]{1,0:T(8,128)S(1)}) fusion(f32[8,8,128]{2,1,0:T(8,128)S(1)} %bitcast.280, f32[8,128]{1,0:T(8,128)S(1)} %get-tuple-element.648, f32[8,8,128]{2,1,0:T(8,128)S(1)} %bitcast.277, f32[8,8,128]{2,1,0:T(8,128)S(1)} %bitcast.279, f32[8,128]{1,0:T(8,128)S(1)} %get-tuple-element.651, ...), kind=kLoop, calls=%fused_computation.58.clone.1 | loop fusion | flops 28308480 | bytes 221440 | tf_op jit(solution)/shard_map/while/body/eval_jaxpr/reduce_sum | solution.py:38
  74.8 5.4 %fusion.116 = (f32[8,128]{1,0:T(8,128)S(1)}, f32[8,128]{1,0:T(8,128)S(1)}, f32[8,128]{1,0:T(8,128)S(1)}) fusion(f32[8,8,128]{2,1,0:T(8,128)S(1)} %bitcast.280, f32[8,128]{1,0:T(8,128)S(1)} %get-tuple-element.648, f32[8,8,128]{2,1,0:T(8,128)S(1)} %bitcast.277, f32[8,8,128]{2,1,0:T(8,128)S(1)} %bitcast.279, f32[8,128]{1,0:T(8,128)S(1)} %get-tuple-element.651, ...), kind=kLoop, calls=%fused_computation.58.clone.1 | loop fusion | flops 28308480 | bytes 221440 | tf_op jit(solution)/shard_map/while/body/eval_jaxpr/reduce_sum | solution.py:38
  80.5 6.2 %collective-permute-done.4 = f32[3,1,32,128]{3,2,1,0:T(8,128)S(1)} collective-permute-done((f32[3,1,32,128]{3,2,1,0:T(8,128)S(1)}, f32[3,1,32,128]{3,2,1,0:T(8,128)S(1)}, u32[]{:S(2)}, u32[]{:S(2)}) %collective-permute-start.4) | collective-permute-done | bytes 49184 | tf_op jit(solution)/shard_map/ppermute | solution.py:17
  86.9 28.9 %while.10 = (s32[]{:T(128)}, f32[4,3,8,128]{3,2,1,0:T(8,128)S(1)}, s32[4,8,8]{2,1,0:T(8,128)S(1)}, f32[3,64,128]{2,0,1:T(4,128)S(1)}, f32[4,3,8,128]{3,2,1,0:T(8...) while((s32[]{:T(128)}, f32[4,3,8,128]{3,2,1,0:T(8,128)S(1)}, ...), condition=%wide.region_14.16_spmd, body=%wide.region_10.15_spmd.sunk | while | flops 28365380 | bytes 1457693 | solution.py:115
  88.7 5.4 %fusion.119 = (f32[8,128]{1,0:T(8,128)S(1)}, f32[8,128]{1,0:T(8,128)S(1)}, f32[8,128]{1,0:T(8,128)S(1)}) fusion(f32[8,8,128]{2,1,0:T(8,128)S(1)} %bitcast.286, f32[8,128]{1,0:T(8,128)S(1)} %get-tuple-element.669, f32[8,8,128]{2,1,0:T(8,128)S(1)} %bitcast.283, f32[8,8,128]{2,1,0:T(8,128)S(1)} %bitcast.285, f32[8,128]{1,0:T(8,128)S(1)} %get-tuple-element.672, ...), kind=kLoop, calls=%fused_computation.94.clone.1 | loop fusion | flops 28308480 | bytes 221440 | tf_op jit(solution)/shard_map/while/body/eval_jaxpr/reduce_sum | solution.py:38
  95.9 5.4 %fusion.119 = (f32[8,128]{1,0:T(8,128)S(1)}, f32[8,128]{1,0:T(8,128)S(1)}, f32[8,128]{1,0:T(8,128)S(1)}) fusion(f32[8,8,128]{2,1,0:T(8,128)S(1)} %bitcast.286, f32[8,128]{1,0:T(8,128)S(1)} %get-tuple-element.669, f32[8,8,128]{2,1,0:T(8,128)S(1)} %bitcast.283, f32[8,8,128]{2,1,0:T(8,128)S(1)} %bitcast.285, f32[8,128]{1,0:T(8,128)S(1)} %get-tuple-element.672, ...), kind=kLoop, calls=%fused_computation.94.clone.1 | loop fusion | flops 28308480 | bytes 221440 | tf_op jit(solution)/shard_map/while/body/eval_jaxpr/reduce_sum | solution.py:38
  103.1 5.4 %fusion.119 = (f32[8,128]{1,0:T(8,128)S(1)}, f32[8,128]{1,0:T(8,128)S(1)}, f32[8,128]{1,0:T(8,128)S(1)}) fusion(f32[8,8,128]{2,1,0:T(8,128)S(1)} %bitcast.286, f32[8,128]{1,0:T(8,128)S(1)} %get-tuple-element.669, f32[8,8,128]{2,1,0:T(8,128)S(1)} %bitcast.283, f32[8,8,128]{2,1,0:T(8,128)S(1)} %bitcast.285, f32[8,128]{1,0:T(8,128)S(1)} %get-tuple-element.672, ...), kind=kLoop, calls=%fused_computation.94.clone.1 | loop fusion | flops 28308480 | bytes 221440 | tf_op jit(solution)/shard_map/while/body/eval_jaxpr/reduce_sum | solution.py:38
  110.4 5.4 %fusion.119 = (f32[8,128]{1,0:T(8,128)S(1)}, f32[8,128]{1,0:T(8,128)S(1)}, f32[8,128]{1,0:T(8,128)S(1)}) fusion(f32[8,8,128]{2,1,0:T(8,128)S(1)} %bitcast.286, f32[8,128]{1,0:T(8,128)S(1)} %get-tuple-element.669, f32[8,8,128]{2,1,0:T(8,128)S(1)} %bitcast.283, f32[8,8,128]{2,1,0:T(8,128)S(1)} %bitcast.285, f32[8,128]{1,0:T(8,128)S(1)} %get-tuple-element.672, ...), kind=kLoop, calls=%fused_computation.94.clone.1 | loop fusion | flops 28308480 | bytes 221440 | tf_op jit(solution)/shard_map/while/body/eval_jaxpr/reduce_sum | solution.py:38
  115.9 6.2 %collective-permute-done.5 = f32[3,1,32,128]{3,2,1,0:T(8,128)S(1)} collective-permute-done((f32[3,1,32,128]{3,2,1,0:T(8,128)S(1)}, f32[3,1,32,128]{3,2,1,0:T(8,128)S(1)}, u32[]{:S(2)}, u32[]{:S(2)}) %collective-permute-start.5) | collective-permute-done | bytes 49184 | tf_op jit(solution)/shard_map/ppermute | solution.py:17
  122.2 6.2 %collective-permute-done.6 = f32[3,1,32,128]{3,2,1,0:T(8,128)S(1)} collective-permute-done((f32[3,1,32,128]{3,2,1,0:T(8,128)S(1)}, f32[3,1,32,128]{3,2,1,0:T(8,128)S(1)}, u32[]{:S(2)}, u32[]{:S(2)}) %collective-permute-start.6) | collective-permute-done | bytes 49184 | tf_op jit(solution)/shard_map/while/body/eval_jaxpr/ppermute | solution.py:17
  128.6 28.9 %while.11 = (s32[]{:T(128)}, f32[4,3,8,128]{3,2,1,0:T(8,128)S(1)}, s32[4,8,8]{2,1,0:T(8,128)S(1)}, f32[3,64,128]{2,0,1:T(4,128)S(1)}, f32[4,3,8,128]{3,2,1,0:T(8...) while((s32[]{:T(128)}, f32[4,3,8,128]{3,2,1,0:T(8,128)S(1)}, ...), condition=%wide.region_19.21_spmd, body=%wide.region_15.20_spmd.sunk | while | flops 28365380 | bytes 1457693 | solution.py:115
  130.4 5.4 %fusion.122 = (f32[8,128]{1,0:T(8,128)S(1)}, f32[8,128]{1,0:T(8,128)S(1)}, f32[8,128]{1,0:T(8,128)S(1)}) fusion(f32[8,8,128]{2,1,0:T(8,128)S(1)} %bitcast.292, f32[8,128]{1,0:T(8,128)S(1)} %get-tuple-element.690, f32[8,8,128]{2,1,0:T(8,128)S(1)} %bitcast.289, f32[8,8,128]{2,1,0:T(8,128)S(1)} %bitcast.291, f32[8,128]{1,0:T(8,128)S(1)} %get-tuple-element.693, ...), kind=kLoop, calls=%fused_computation.130.clone.1 | loop fusion | flops 28308480 | bytes 221440 | tf_op jit(solution)/shard_map/while/body/eval_jaxpr/reduce_sum | solution.py:38
  137.7 5.4 %fusion.122 = (f32[8,128]{1,0:T(8,128)S(1)}, f32[8,128]{1,0:T(8,128)S(1)}, f32[8,128]{1,0:T(8,128)S(1)}) fusion(f32[8,8,128]{2,1,0:T(8,128)S(1)} %bitcast.292, f32[8,128]{1,0:T(8,128)S(1)} %get-tuple-element.690, f32[8,8,128]{2,1,0:T(8,128)S(1)} %bitcast.289, f32[8,8,128]{2,1,0:T(8,128)S(1)} %bitcast.291, f32[8,128]{1,0:T(8,128)S(1)} %get-tuple-element.693, ...), kind=kLoop, calls=%fused_computation.130.clone.1 | loop fusion | flops 28308480 | bytes 221440 | tf_op jit(solution)/shard_map/while/body/eval_jaxpr/reduce_sum | solution.py:38
  144.9 5.4 %fusion.122 = (f32[8,128]{1,0:T(8,128)S(1)}, f32[8,128]{1,0:T(8,128)S(1)}, f32[8,128]{1,0:T(8,128)S(1)}) fusion(f32[8,8,128]{2,1,0:T(8,128)S(1)} %bitcast.292, f32[8,128]{1,0:T(8,128)S(1)} %get-tuple-element.690, f32[8,8,128]{2,1,0:T(8,128)S(1)} %bitcast.289, f32[8,8,128]{2,1,0:T(8,128)S(1)} %bitcast.291, f32[8,128]{1,0:T(8,128)S(1)} %get-tuple-element.693, ...), kind=kLoop, calls=%fused_computation.130.clone.1 | loop fusion | flops 28308480 | bytes 221440 | tf_op jit(solution)/shard_map/while/body/eval_jaxpr/reduce_sum | solution.py:38
  (257 shorter events, 43.4 us)
Async XLA Ops:
  0.6 7.6 %copy-start.3 = (f32[1,128]{1,0:T(1,128)S(1)}, f32[1,128]{1,0:T(1,128)}, u32[]{:S(2)}) copy-start(f32[1,128]{1,0:T(1,128)} %param.18) | copy-start | bytes 1540
  0.6 7.6 %collective-permute-start = (f32[3,1,32,128]{3,2,1,0:T(8,128)}, f32[3,1,32,128]{3,2,1,0:T(8,128)S(1)}, u32[]{:S(2)}, u32[]{:S(2)}) collective-permute-start(f32[3,1,32,128]{3,2,1,0:T(8,128)} %param.16), channel_id=1, source_target_pairs={{15,0},{0,1},{1,2},{2,3},{3,4},{4,5},{5,6},{6,7},{7,8},{8,9},{9,10... | collective-permute-start | bytes 147464 | tf_op jit(solution)/shard_map/ppermute | solution.py:17
  1.1 7.0 %collective-permute-start.1 = (f32[1,128]{1,0:T(1,128)}, f32[1,128]{1,0:T(1,128)S(1)}, u32[]{:S(2)}, u32[]{:S(2)}) collective-permute-start(f32[1,128]{1,0:T(1,128)} %param.18), channel_id=1, source_target_pairs={{15,0},{0,1},{1,2},{2,3},{3,4},{4,5},{5,6},{6,7},{7,8},{8,9},{9,10... | collective-permute-start | bytes 1544 | tf_op jit(solution)/shard_map/while/body/eval_jaxpr/ppermute | solution.py:17
  8.4 0.8 copy-start
  9.2 29.3 %copy-start.2 = (f32[3]{0:T(128)S(1)}, f32[3]{0:T(128)}, u32[]{:S(2)}) copy-start(f32[3]{0:T(128)} %constant.176.clone) | copy-start | bytes 40
  9.2 35.6 %copy-start.1 = (f32[3,1,128]{2,1,0:T(1,128)S(1)}, f32[3,1,128]{2,1,0:T(1,128)}, u32[]{:S(2)}) copy-start(f32[3,1,128]{2,1,0:T(1,128)} %param.17) | copy-start | bytes 4612
  38.6 6.2 %collective-permute-start.2 = (f32[3,1,32,128]{3,2,1,0:T(8,128)S(1)}, f32[3,1,32,128]{3,2,1,0:T(8,128)S(1)}, u32[]{:S(2)}, u32[]{:S(2)}) collective-permute-start(f32[3,1,32,128]{3,2,1,0:T(8,128)S(1)} %bitcast_add_fusion.3), channel_id=1, source_target_pairs={{15,0},{0,1},{1,2},{2,3},{3,4},{4,5},{5,6},{6,7},{7,8},{8,9},{9,10... | collective-permute-start | bytes 147464 | tf_op jit(solution)/shard_map/ppermute | solution.py:17
  44.8 6.3 %collective-permute-start.3 = (f32[3,1,32,128]{3,2,1,0:T(8,128)S(1)}, f32[3,1,32,128]{3,2,1,0:T(8,128)S(1)}, u32[]{:S(2)}, u32[]{:S(2)}) collective-permute-start(f32[3,1,32,128]{3,2,1,0:T(8,128)S(1)} %multiply_add_fusion.2), channel_id=1, source_target_pairs={{15,0},{0,1},{1,2},{2,3},{3,4},{4,5},{5,6},{6,7},{7,8},{8,9},{9,10... | collective-permute-start | bytes 147464 | tf_op jit(solution)/shard_map/while/body/eval_jaxpr/ppermute | solution.py:17
  80.4 6.3 %collective-permute-start.4 = (f32[3,1,32,128]{3,2,1,0:T(8,128)S(1)}, f32[3,1,32,128]{3,2,1,0:T(8,128)S(1)}, u32[]{:S(2)}, u32[]{:S(2)}) collective-permute-start(f32[3,1,32,128]{3,2,1,0:T(8,128)S(1)} %fusion.72), channel_id=1, source_target_pairs={{15,0},{0,1},{1,2},{2,3},{3,4},{4,5},{5,6},{6,7},{7,8},{8,9},{9,10... | collective-permute-start | bytes 147464 | tf_op jit(solution)/shard_map/ppermute | solution.py:17
  115.9 6.2 %collective-permute-start.5 = (f32[3,1,32,128]{3,2,1,0:T(8,128)S(1)}, f32[3,1,32,128]{3,2,1,0:T(8,128)S(1)}, u32[]{:S(2)}, u32[]{:S(2)}) collective-permute-start(f32[3,1,32,128]{3,2,1,0:T(8,128)S(1)} %bitcast_add_fusion.1), channel_id=1, source_target_pairs={{15,0},{0,1},{1,2},{2,3},{3,4},{4,5},{5,6},{6,7},{7,8},{8,9},{9,10... | collective-permute-start | bytes 147464 | tf_op jit(solution)/shard_map/ppermute | solution.py:17
  122.1 6.3 %collective-permute-start.6 = (f32[3,1,32,128]{3,2,1,0:T(8,128)S(1)}, f32[3,1,32,128]{3,2,1,0:T(8,128)S(1)}, u32[]{:S(2)}, u32[]{:S(2)}) collective-permute-start(f32[3,1,32,128]{3,2,1,0:T(8,128)S(1)} %multiply_add_fusion.1), channel_id=1, source_target_pairs={{15,0},{0,1},{1,2},{2,3},{3,4},{4,5},{5,6},{6,7},{7,8},{8,9},{9,10... | collective-permute-start | bytes 147464 | tf_op jit(solution)/shard_map/while/body/eval_jaxpr/ppermute | solution.py:17
where the time goes:
time: 159 us; the launch traced here: 158 us
  other arithmetic  93.3 us (59%)
  waiting for transfers between devices  31.8 us (20%)
  local copies, waits for them, and re-layouts  27.6 us (17%)
  starting transfers between devices  3.31 us (2%)
    reduce_sum x16, other arithmetic, induce(): jnp.sum((lever_two * delta_three - lever_three * delta_two) * weight, axi...  87.1 us
    ppermute x7, waiting for transfers between devices, shifted(): return lax.ppermute(block, axis, route)  31.8 us
    gather x16, local copies, waits for them, and re-layouts, one_block(): jnp.take(flat_lever, picked.reshape(-1), axis=1)  10.5 us
    gather x16, local copies, waits for them, and re-layouts, one_block(): jnp.take(flat_mid, picked.reshape(-1), axis=1)  10.5 us
    ppermute x7, starting transfers between devices, shifted(): return lax.ppermute(block, axis, route)  3.31 us
  transfers between devices with their start and end apart: 7, of which 6 were waited for; matrix products, arithmetic and copies ran while one was open for 2% of the time, Pallas kernels for 0%

commit v1 on v0

v1 whole, which is shorter than its diff:
```python
import functools
import math

import jax
import jax.numpy as jnp
from jax import lax
from jax.experimental import pallas as pl
from jax.experimental.pallas import tpu as pltpu
from jax.sharding import PartitionSpec as P

SWEEPS = 2
STEP = 0.05
core_square = 0.01
NODES = 128
GROUP = 4
MESH = pl.DeviceIdType.MESH


def split_three(value):
    first = value.astype(jnp.bfloat16).astype(jnp.float32)
    rest = value - first
    second = rest.astype(jnp.bfloat16).astype(jnp.float32)
    return first, second, rest - second


def velocity_of(
    ages,
    slots,
    blocks,
    centre,
    picked,
    raw_target,
    raw_source,
    raw_lever,
    target_tab,
    source_tab,
    lever_tab,
    sum_tab,
    result_tab,
):
    zeros = jnp.zeros((ages, NODES), jnp.float32)
    ones = jnp.ones((ages, NODES), jnp.float32)
    row = lax.broadcasted_iota(jnp.int32, (ages, NODES), 0)

    def rows_of(tile, k):
        return pl.ds(tile * 8 + k, ages, stride=8)

    for k in range(5, 8):
        raw_target[rows_of(0, k), :] = zeros
        for block in range(blocks):
            raw_source[rows_of(block * ages, k), :] = zeros
    raw_target[rows_of(0, 3), :] = ones
    for block in range(blocks):
        raw_source[rows_of(block * ages, 4), :] = ones
        for k in range(6, 8):
            raw_lever[rows_of(block * ages, k), :] = zeros
    source_tab[blocks * ages] = jnp.zeros(source_tab.shape[1:], jnp.bfloat16)
    lever_tab[blocks * ages] = jnp.zeros(lever_tab.shape[1:], jnp.bfloat16)

    def velocity(fields, strengths, target):
        moved = [target[c] - centre[c] for c in range(3)]
        for c in range(3):
            raw_target[rows_of(0, c), :] = moved[c]
        raw_target[rows_of(0, 4), :] = (
            moved[0] * moved[0] + moved[1] * moved[1] + moved[2] * moved[2]
        )
        for block in range(blocks):
            coords = [fields[block][c] - centre[c] for c in range(3)]
            following = [
                jnp.where(row == ages - 1, q, pltpu.roll(q, ages - 1, 0)) for q in coords
            ]
            gain = strengths[block] * (0.25 / math.pi)
            mid = [0.5 * (q + f) for q, f in zip(coords, following)]
            lev = [(f - q) * gain for q, f in zip(coords, following)]
            base = block * ages
            for c in range(3):
                raw_source[rows_of(base, c), :] = -2.0 * mid[c]
                raw_lever[rows_of(base, c), :] = lev[c]
                d, e = (c + 1) % 3, (c + 2) % 3
                raw_lever[rows_of(base, 3 + c), :] = lev[d] * mid[e] - lev[e] * mid[d]
            raw_source[rows_of(base, 3), :] = (
                mid[0] * mid[0] + mid[1] * mid[1] + mid[2] * mid[2] + core_square
            )

        def prepare_sources(tile):
            at = pl.ds(pl.multiple_of(tile * 8, 8), 8)
            one, two, three = split_three(raw_source[at, :])
            source_tab[tile] = jnp.concatenate(
                [one, two, three, one, two, one], axis=0
            ).astype(jnp.bfloat16)
            one, two, three = split_three(raw_lever[at, :])
            lever_tab[tile] = jnp.concatenate(
                [one, two, three, jnp.zeros_like(one)], axis=0
            ).astype(jnp.bfloat16)

        def prepare_targets(tile):
            at = pl.ds(pl.multiple_of(tile * 8, 8), 8)
            one, two, three = split_three(raw_target[at, :])
            pile = jnp.concatenate(
                [one, one, one, two, two, three, jnp.zeros((NODES - 48, NODES), jnp.float32)],
                axis=0,
            )
            target_tab[tile] = pile.T.astype(jnp.bfloat16)

        def prepare(i, carry):
            for u in range(8):
                prepare_sources(i * 8 + u)
            return carry

        def prepare_both(i, carry):
            for u in range(4):
                prepare_targets(i * 4 + u)
            return prepare(i, carry)

        lax.fori_loop(0, ages // 4, prepare_both, 0)
        if blocks > 2:
            lax.fori_loop(ages // 4, blocks * ages // 8, prepare, 0)

        def one_tile(tile):
            total = None
            left = target_tab[tile][:, :48]
            for slot in range(0, slots, 2):
                first, second = picked(tile, slot), picked(tile, slot + 1)
                right = jnp.concatenate([source_tab[first], source_tab[second]], axis=1)
                square = jnp.dot(left, right, preferred_element_type=jnp.float32)
                inverse = lax.rsqrt(jnp.maximum(square, core_square))
                weight = inverse * inverse * inverse
                high = weight.astype(jnp.bfloat16)
                low = (weight - high.astype(jnp.float32)).astype(jnp.bfloat16)
                levers = jnp.concatenate([lever_tab[first], lever_tab[second]], axis=1)
                term = lax.dot_general(
                    jnp.concatenate([high, low], axis=0),
                    levers,
                    (((1,), (1,)), ((), ())),
                    preferred_element_type=jnp.float32,
                )
                total = term if total is None else total + term
            sum_tab[tile, :, :32] = total[:NODES] + total[NODES:]

        def tiles(i, carry):
            for u in range(GROUP):
                one_tile(i * GROUP + u)
            return carry

        lax.fori_loop(0, ages // GROUP, tiles, 0)

        def finish(i, carry):
            for u in range(4):
                tile = i * 4 + u
                flat = sum_tab[tile].T
                at = pl.ds(pl.multiple_of(tile * 8, 8), 8)
                result_tab[at, :] = flat[0:8] + flat[8:16] + flat[16:24]
            return carry

        lax.fori_loop(0, ages // 4, finish, 0)
        total = [result_tab[rows_of(0, k), :] for k in range(6)]
        swirl = []
        for c in range(3):
            d, e = (c + 1) % 3, (c + 2) % 3
            swirl.append(total[d] * moved[e] - total[e] * moved[d] - total[3 + c])
        swirl[2] = swirl[2] - 0.2
        return swirl

    sum_tab[...] = jnp.zeros_like(sum_tab)
    return velocity


def table_shapes(ages, blocks):
    f32, bf16 = jnp.float32, jnp.bfloat16
    return [
        pltpu.VMEM((ages * 8, NODES), f32),
        pltpu.VMEM((blocks * ages * 8, NODES), f32),
        pltpu.VMEM((blocks * ages * 8, NODES), f32),
        pltpu.VMEM((ages, NODES, NODES), bf16),
        pltpu.VMEM((blocks * ages + 1, 48, NODES), bf16),
        pltpu.VMEM((blocks * ages + 1, 32, NODES), bf16),
        pltpu.VMEM((ages, NODES, NODES), f32),
        pltpu.VMEM((ages * 8, NODES), f32),
    ]


def relax_kernel(
    device_count,
    ages,
    slots,
    wake_ref,
    release_ref,
    strength_ref,
    list_ref,
    count_ref,
    relaxed_ref,
    induced_ref,
    own_ref,
    got_ref,
    edge_ref,
    edge_strength_ref,
    pred_ref,
    send_sem,
    recv_sem,
    edge_send,
    edge_recv,
    *tables,
):
    me = lax.axis_index("azim")
    cases = lax.axis_index("cases")

    def ahead(distance):
        return (cases, lax.rem(me + distance + device_count, device_count))

    barrier = pltpu.get_barrier_semaphore()
    for distance in (1, 2, -1, -2):
        pl.semaphore_signal(barrier, inc=1, device_id=ahead(distance), device_id_type=MESH)
    pl.semaphore_wait(barrier, 4)

    def send(round_index, source):
        copies = [
            pltpu.make_async_remote_copy(
                src_ref=source,
                dst_ref=got_ref.at[round_index, hop],
                send_sem=send_sem.at[round_index, hop],
                recv_sem=recv_sem.at[round_index, hop],
                device_id=ahead(hop + 1),
                device_id_type=MESH,
            )
            for hop in range(2)
        ]
        for copy in copies:
            copy.start()
        return copies

    edges = [
        pltpu.make_async_remote_copy(
            src_ref=source,
            dst_ref=target,
            send_sem=edge_send.at[i],
            recv_sem=edge_recv.at[i],
            device_id=ahead(1),
            device_id_type=MESH,
        )
        for i, (source, target) in enumerate(
            ((release_ref, edge_ref), (strength_ref, edge_strength_ref))
        )
    ]
    own_ref[0] = wake_ref[:, 0]
    pending = send(0, own_ref.at[0])
    for copy in edges:
        copy.start()

    row = lax.broadcasted_iota(jnp.int32, (ages, NODES), 0)
    centre = [jnp.sum(wake_ref[c, 0]) * (1.0 / (ages * NODES)) for c in range(3)]

    def picked(tile, slot):
        ident = list_ref[0, tile, slot]
        column = ident // ages
        local = jnp.where(column == me, 0, ages) + ident % ages
        return jnp.where(slot < count_ref[0, tile], local, 2 * ages)

    velocity = velocity_of(ages, slots, 2, centre, picked, *tables)

    def back(field, edge):
        return jnp.where(row == 0, edge, pltpu.roll(field, 1, 0))

    def receive(copies):
        for copy in copies:
            copy.wait()

    strength_own = strength_ref[...]
    receive(pending)
    for copy in edges:
        copy.wait()
    strengths = (strength_own, edge_strength_ref[...])

    for sweep in range(SWEEPS):
        at_pos, at_speed = 2 * sweep, 2 * sweep + 1
        position = [own_ref[at_pos, c] for c in range(3)]
        behind = [got_ref[at_pos, 0, c] for c in range(3)]
        speed = velocity((position, behind), strengths, position)
        for c in range(3):
            own_ref[at_speed, c] = speed[c]
        receive(send(at_speed, own_ref.at[at_speed]))
        for block in range(2):
            for c in range(3):
                edge = release_ref[c] if block == 0 else edge_ref[c]
                pred_ref[block, c] = back(got_ref[at_pos, block, c], edge) + STEP * back(
                    got_ref[at_speed, block, c], 0.0
                )
        predicted = [[pred_ref[block, c] for c in range(3)] for block in range(2)]
        induced = velocity(predicted, strengths, predicted[0])
        for c in range(3):
            back_pos = back(got_ref[at_pos, 0, c], release_ref[c])
            back_speed = back(got_ref[at_speed, 0, c], 0.0)
            corrected = back_pos + 0.5 * STEP * (back_speed + induced[c])
            old = own_ref[at_pos, c]
            new = old + 0.5 * (corrected - old)
            if sweep == SWEEPS - 1:
                relaxed_ref[c, 0] = new
                induced_ref[c, 0] = induced[c]
            else:
                own_ref[at_pos + 2, c] = new
        if sweep < SWEEPS - 1:
            receive(send(at_pos + 2, own_ref.at[at_pos + 2]))


def relax_near(device_count, wake, release, strength, source_list, list_count):
    ages, slots = wake.shape[2], source_list.shape[2]
    rounds = 2 * SWEEPS
    f32 = jnp.float32
    vmem = pl.BlockSpec(memory_space=pltpu.VMEM)
    smem = pl.BlockSpec(memory_space=pltpu.SMEM)
    field = (3, ages, NODES)
    return pl.pallas_call(
        functools.partial(relax_kernel, device_count, ages, slots),
        out_shape=(
            jax.ShapeDtypeStruct(wake.shape, f32),
            jax.ShapeDtypeStruct(wake.shape, f32),
        ),
        in_specs=[vmem, vmem, vmem, smem, smem],
        out_specs=(vmem, vmem),
        scratch_shapes=[
            pltpu.VMEM((rounds,) + field, f32),
            pltpu.VMEM((rounds, 2) + field, f32),
            pltpu.VMEM(release.shape, f32),
            pltpu.VMEM(strength.shape, f32),
            pltpu.VMEM((2,) + field, f32),
            pltpu.SemaphoreType.DMA((rounds, 2)),
            pltpu.SemaphoreType.DMA((rounds, 2)),
            pltpu.SemaphoreType.DMA((2,)),
            pltpu.SemaphoreType.DMA((2,)),
            *table_shapes(ages, 2),
        ],
        compiler_params=pltpu.CompilerParams(
            collective_id=0, has_side_effects=True, vmem_limit_bytes=32 * 2**20
        ),
    )(wake, release, strength, source_list, list_count)


def induce_kernel(ages, slots, blocks, target_ref, window_ref, strength_ref, pick_ref, out_ref, *tables):
    centre = [jnp.sum(target_ref[c, 0]) * (1.0 / (ages * NODES)) for c in range(3)]
    velocity = velocity_of(
        ages, slots, blocks, centre, lambda tile, slot: pick_ref[tile * slots + slot], *tables
    )
    fields = [[window_ref[c, block] for c in range(3)] for block in range(blocks)]
    strengths = [strength_ref[block : block + 1, :] for block in range(blocks)]
    target = [target_ref[c, 0] for c in range(3)]
    for c, part in enumerate(velocity(fields, strengths, target)):
        out_ref[c, 0] = part


def induce_window(coords, window, window_strength, picks, slots):
    ages, blocks = coords.shape[2], window.shape[1]
    vmem = pl.BlockSpec(memory_space=pltpu.VMEM)
    return pl.pallas_call(
        functools.partial(induce_kernel, ages, slots, blocks),
        out_shape=jax.ShapeDtypeStruct(coords.shape, jnp.float32),
        in_specs=[vmem, vmem, vmem, pl.BlockSpec(memory_space=pltpu.SMEM)],
        out_specs=vmem,
        scratch_shapes=table_shapes(ages, blocks),
        compiler_params=pltpu.CompilerParams(vmem_limit_bytes=48 * 2**20),
    )(coords, window, window_strength, picks)


def shifted(block, axis, distance):
    devices = range(lax.axis_size(axis))
    route = [((i - distance) % len(devices), i) for i in devices]
    return lax.ppermute(block, axis, route)


def shift_local(coords, edge_pos, boundary):
    rolled = jnp.concatenate([edge_pos, coords[:, :-1]], axis=1)
    return jnp.concatenate([boundary[:, :, None, :], rolled[:, :, :-1, :]], axis=2)


def gather_window(coords, strength, reach_blocks):
    psi_local = coords.shape[1]
    if reach_blocks > 1:
        first_block = shifted((coords, strength), "azim", -(reach_blocks - 1))
    else:
        first_block = (coords, strength)
    width_cols = 2 * reach_blocks * psi_local
    pos_buffer = jnp.zeros((3, width_cols) + coords.shape[2:], jnp.float32)
    str_buffer = jnp.zeros((width_cols, strength.shape[1]), jnp.float32)
    pos_buffer = lax.dynamic_update_slice_in_dim(pos_buffer, first_block[0], 0, axis=1)
    str_buffer = lax.dynamic_update_slice_in_dim(str_buffer, first_block[1], 0, axis=0)

    def advance(hop_index, carry):
        current, pos_now, str_now = carry
        current = shifted((current[0], current[1]), "azim", 1)
        pos_now = lax.dynamic_update_slice_in_dim(
            pos_now, current[0], hop_index * psi_local, axis=1
        )
        str_now = lax.dynamic_update_slice_in_dim(
            str_now, current[1], hop_index * psi_local, axis=0
        )
        return (current, pos_now, str_now)

    result = lax.fori_loop(1, 2 * reach_blocks, advance, (first_block, pos_buffer, str_buffer))
    return (result[1], result[2])


def on_device(wake, release, strength, source_list, list_count):
    device_count = lax.axis_size("azim")
    reach_blocks = device_count // 16
    if reach_blocks == 1 and wake.shape[1] == 1:
        return relax_near(device_count, wake, release, strength, source_list, list_count)
    own_index = lax.axis_index("azim")
    psi_local = wake.shape[1]
    age_count = wake.shape[2]
    slot_count = source_list.shape[2]
    column = source_list // age_count
    age_part = source_list % age_count
    owner_block = column // psi_local
    within = column % psi_local
    offset = (owner_block - own_index + reach_blocks) % device_count - reach_blocks
    local_ids = ((reach_blocks - 1 - offset) * psi_local + within) * age_count + age_part
    used = jnp.arange(slot_count, dtype=jnp.int32) < list_count[:, :, None]
    empty = 2 * reach_blocks * psi_local * age_count
    picks = jnp.where(used, local_ids, empty).reshape(-1)

    def velocity(coords):
        win_pos, win_str = gather_window(coords, strength, reach_blocks)
        return induce_window(coords, win_pos, win_str, picks, slot_count)

    positions = wake
    induced = jnp.zeros_like(wake)
    for sweep_index in range(SWEEPS):
        speed_now = velocity(positions)
        edge_pos, edge_speed = shifted((positions, speed_now), "azim", 1)
        back_pos = shift_local(positions, edge_pos, release)
        back_speed = shift_local(speed_now, edge_speed, jnp.zeros_like(release))
        predicted = back_pos + 0.05 * back_speed
        induced = velocity(predicted)
        corrected = back_pos + 0.025 * (back_speed + induced)
        positions = positions + 0.5 * (corrected - positions)
    return (positions, induced)


def solution(mesh):
    placed = (
        P(None, ("cases", "azim"), None, None),
        P(None, ("cases", "azim"), None),
        P(("cases", "azim"), None),
        P(("cases", "azim"), None, None),
        P(("cases", "azim"), None),
    )
    return jax.shard_map(
        on_device,
        mesh=mesh,
        in_specs=placed,
        out_specs=(P(None, ("cases", "azim"), None, None), P(None, ("cases", "azim"), None, None)),
        check_vma=False,
    )
```

time: 159 us -> 76.3 us (0.48)
  other arithmetic: 93.3 us -> 0 us
  Pallas kernels: 0 us -> 72.6 us
  waiting for transfers between devices: 31.8 us -> 0 us
  local copies, waits for them, and re-layouts: 27.6 us -> 2.83 us
  starting transfers between devices: 3.31 us -> 0 us
    reduce_sum x16 -> x0, other arithmetic: 87.1 us -> none  [induce(): jnp.sum((lever_two * delta_three - lever_three * delta_two) * weight, axi...]
    pallas_call x0 -> x1, Pallas kernels: none -> 72.6 us  [relax_near(): pl.pallas_call(functools.partial(relax_kernel, device_count, ages, slots)...]
    ppermute x7 -> x0, waiting for transfers between devices: 31.8 us -> none  [shifted(): return lax.ppermute(block, axis, route)]
    gather x32 -> x0, local copies, waits for them, and re-layouts: 21 us -> none  [the longest x16 10.5 us: one_block(): jnp.take(flat_lever, picked.reshape(-1), axis=1)]
    ppermute x7 -> x0, starting transfers between devices: 3.31 us -> none  [shifted(): return lax.ppermute(block, axis, route)]
    select_n x32 -> x0, other arithmetic: 2.27 us -> none  [one_block(): jnp.take(flat_lever, picked.reshape(-1), axis=1)]
    slice x18 -> x0, local copies, waits for them, and re-layouts: 2.22 us -> none  [the longest x16 2.21 us: induce(): lever_one = levers[0][:, :, None, :]]
    add x7 -> x0, other arithmetic: 1.7 us -> none  [the longest x2 0.8 us: on_device(): positions = positions + 0.5 * (corrected - positions)]
  transfers between devices with their start and end apart: 7 -> 0, of which waited for: 6 -> 0; matrix products, arithmetic and copies ran while one was open for 2% -> 0% of each run, Pallas kernels for 0% -> 0%
where the time goes in v1:
time: 76.3 us; the launch traced here: 76.1 us
  Pallas kernels  72.6 us (95%)
  local copies, waits for them, and re-layouts  2.83 us (4%)
    pallas_call x1, Pallas kernels, relax_near(): pl.pallas_call(functools.partial(relax_kernel, device_count, ages, slots)...  72.6 us
    unnamed x11, local copies, waits for them, and re-layouts  2.83 us

profile of v1, /device:TPU:0, one launch (start us, length us, event | category | flops | bytes accessed | tf_op | source)
XLA Modules:
  0.0 76.1 jit_solution(6057458483621297332)
XLA Ops:
  0.6 0.0 copy-start.3
  0.6 0.0 copy-start.2
  0.7 0.0 copy-start.1
  0.7 0.8 %copy.7.list_ref = s32[1,32,8]{2,1,0:T(8,128)S(1)} copy(s32[1,32,8]{1,2,0:T(8,128)} %param.8) | data formatting | bytes 2048 | tf_op args[3]
  1.4 0.0 copy-done.3
  1.4 0.0 copy-done.2
  1.4 0.0 copy-done.1
  1.5 0.0 copy-start
  1.5 0.8 %copy-done = f32[3,1,32,128]{3,2,1,0:T(8,128)S(1)} copy-done((f32[3,1,32,128]{3,2,1,0:T(8,128)S(1)}, f32[3,1,32,128]{3,2,1,0:T(8,128)}, u32[]{:S(2)}) %copy-start) | copy-done | bytes 49176
  2.3 72.6 %shard_map.68 = (f32[3,1,32,128]{3,2,1,0:T(8,128)S(1)}, f32[3,1,32,128]{3,2,1,0:T(8,128)S(1)}) custom-call(f32[3,1,32,128]{3,2,1,0:T(8,128)S(1)} %copy-done, f32[3,1,128]{2,1,0:T(1,128)S(1)} %copy-done.1, f32[1,128]{1,0:T(1,128)S(1)} %copy-done.2, s32[1,32,8]{2,1,0:T(8,128)S(1)} %copy.7.list_ref, s32[1,32]{1,0:T(1,128)S(1)} %copy-done.3), custom_call_target="tpu_custom_call" | custom-call | tf_op jit(solution)/shard_map/pallas_call | solution.py:311
  74.9 0.6 copy.10
  75.5 0.6 copy.11
Async XLA Ops:
  0.6 0.8 %copy-start.3 = (s32[1,32]{1,0:T(1,128)S(1)}, s32[1,32]{1,0:T(1,128)}, u32[]{:S(2)}) copy-start(s32[1,32]{1,0:T(1,128)} %count_ref.1) | copy-start | bytes 388
  0.6 0.8 %copy-start.2 = (f32[1,128]{1,0:T(1,128)S(1)}, f32[1,128]{1,0:T(1,128)}, u32[]{:S(2)}) copy-start(f32[1,128]{1,0:T(1,128)} %strength_ref.1) | copy-start | bytes 1540
  0.7 0.8 %copy-start.1 = (f32[3,1,128]{2,1,0:T(1,128)S(1)}, f32[3,1,128]{2,1,0:T(1,128)}, u32[]{:S(2)}) copy-start(f32[3,1,128]{2,1,0:T(1,128)} %release_ref.1) | copy-start | bytes 4612
  1.5 0.8 %copy-start = (f32[3,1,32,128]{3,2,1,0:T(8,128)S(1)}, f32[3,1,32,128]{3,2,1,0:T(8,128)}, u32[]{:S(2)}) copy-start(f32[3,1,32,128]{3,2,1,0:T(8,128)} %wake_ref.1) | copy-start | bytes 147460
